TPU v7x, 256 devices: a whole 4x4x8 slice. The times are simulated.
256 devices in a mesh: clus: 16 (over z, core), node: 16 (over x, y).
Axes of the slice: x: 4, y: 4, z: 8, core: 2. Of those that a mesh axis runs over, the one named last changes fastest.
Arguments:
- node_feats: bfloat16 [16, 2048, 1024], P('clus', 'node'), may hold values from -6 to 6
- cotangent: bfloat16 [16, 2048, 1024], P('clus', 'node'), may hold values from -6 to 6
- w_query: bfloat16 [1024, 1024], replicated, may hold values from -0.1875 to 0.1875
- w_key: bfloat16 [1024, 1024], replicated, may hold values from -0.1875 to 0.1875
- w_value: bfloat16 [1024, 1024], replicated, may hold values from -0.1875 to 0.1875
- w_out: bfloat16 [1024, 1024], replicated, may hold values from -0.1875 to 0.1875
- eigvec: bfloat16 [16, 64, 2048], P('clus'), may hold values from -3.5 to 3.5
- eig_weight: float32 [16, 64], P('node'), may hold values from 0.1 to 1
- block_mask: int32 [16, 16, 16, 16], P('clus', 'node'), may hold values from 0 to 1, as said below
Outputs:
- grad_nodes: bfloat16 [16, 2048, 1024], P('clus', 'node')
- grad_eigvec: float32 [16, 64, 2048], P('clus', None, 'node')
- grad_weight: float32 [16, 64], P('node')
- grad_proj: float32 [4, 1024, 1024], P(None, 'clus', 'node')
Inputs may be any that keep to these rules, and one draw needn't show every extreme that they name: `block_mask`: each entry is 0 or 1; every diagonal tile is 1; the share of present tiles differs between clusters and heads.
All inputs are finite; a program needn't handle non-finite values.
Results may differ from a plain program's by a relative error of at most 0.012.
The roundings to bfloat16 on the way count: a program that leaves them out, or rounds other values in their place, can miss the bound.
Values may be sent and summed in bfloat16 or wider, within the bound.
A program may use at most 128 MiB of HBM per device.

v0:
```python
import jax
import jax.numpy as jnp
from jax import lax
from jax.sharding import PartitionSpec as P


def body(node_feats, cotangent, w_query, w_key, w_value, w_out, eigvec, eig_weight, block_mask):
    node_rows = node_feats[0]
    grads_in = cotangent[0]
    query = jnp.dot(node_rows, w_query, preferred_element_type=jnp.float32).astype(jnp.bfloat16)
    keys_local = jnp.dot(node_rows, w_key, preferred_element_type=jnp.float32).astype(jnp.bfloat16)
    values_local = jnp.dot(node_rows, w_value, preferred_element_type=jnp.float32).astype(
        jnp.bfloat16
    )
    d_att = jnp.dot(grads_in, w_out, preferred_element_type=jnp.float32).astype(jnp.bfloat16)
    head_data = lax.all_to_all(
        jnp.stack([query, keys_local, values_local, d_att]),
        "node",
        split_axis=2,
        concat_axis=1,
        tiled=True,
    )
    node_count = head_data.shape[1]
    head_width = head_data.shape[2]
    heads_dev = eig_weight.shape[0]
    head_size = head_width // heads_dev
    by_head = head_data.reshape(4, node_count, heads_dev, head_size)
    query_heads = by_head[0]
    keys_heads = by_head[1]
    values_heads = by_head[2]
    dout_heads = by_head[3]
    eig_all = eigvec[0]
    eig_float = eig_all.astype(jnp.float32)
    weighted = (eig_weight[:, :, None] * eig_float[None]).astype(jnp.bfloat16)
    tile_mask = block_mask[0]
    tile_count = tile_mask.shape[2]
    tile_size = node_count // tile_count
    block_rows = min(512, node_count)
    block_count = node_count // block_rows
    score_scale = head_size ** (-0.5)

    def one_block(totals, block_index):
        key_grad, value_grad, eig_right, weight_grad = totals
        offset = block_index * block_rows
        query_block = lax.dynamic_slice_in_dim(query_heads, offset, block_rows, 0)
        dout_block = lax.dynamic_slice_in_dim(dout_heads, offset, block_rows, 0)
        eig_block = lax.dynamic_slice_in_dim(eig_all, offset, block_rows, 1)
        eig_bias = jnp.einsum(
            "ki,hkj->hij", eig_block, weighted, preferred_element_type=jnp.float32
        )
        scores = (
            jnp.einsum("ihd,jhd->hij", query_block, keys_heads, preferred_element_type=jnp.float32)
            * score_scale
            + eig_bias
        )
        tile_rows = lax.dynamic_slice_in_dim(
            tile_mask, offset // tile_size, block_rows // tile_size, 1
        )
        present = jnp.broadcast_to(
            tile_rows[:, :, None, :, None] > 0,
            (heads_dev, block_rows // tile_size, tile_size, tile_count, tile_size),
        )
        present = present.reshape(heads_dev, block_rows, node_count)
        masked = jnp.where(present, scores, -jnp.inf)
        row_max = jnp.max(masked, axis=2, keepdims=True)
        raised = jnp.exp(masked - row_max)
        attn_prob = raised / jnp.sum(raised, axis=2, keepdims=True)
        prob_half = attn_prob.astype(jnp.bfloat16)
        out_block = jnp.einsum(
            "hij,jhd->ihd", prob_half, values_heads, preferred_element_type=jnp.float32
        ).astype(jnp.bfloat16)
        dprob = jnp.einsum(
            "ihd,jhd->hij", dout_block, values_heads, preferred_element_type=jnp.float32
        )
        row_delta = jnp.sum(attn_prob * dprob, axis=2, keepdims=True)
        dscore = (attn_prob * (dprob - row_delta)).astype(jnp.bfloat16)
        query_grad = (
            jnp.einsum("hij,jhd->ihd", dscore, keys_heads, preferred_element_type=jnp.float32)
            * score_scale
        ).astype(jnp.bfloat16)
        key_grad = key_grad + jnp.einsum(
            "hij,ihd->jhd", dscore, query_block, preferred_element_type=jnp.float32
        )
        value_grad = value_grad + jnp.einsum(
            "hij,ihd->jhd", prob_half, dout_block, preferred_element_type=jnp.float32
        )
        eig_left = jnp.einsum("hij,kj->hki", dscore, eig_all, preferred_element_type=jnp.float32)
        weight_grad = weight_grad + jnp.sum(eig_left * eig_block.astype(jnp.float32)[None], axis=2)
        eig_right = eig_right + jnp.einsum(
            "hij,ki->hkj", dscore, eig_block, preferred_element_type=jnp.float32
        )
        left_term = jnp.sum(eig_weight[:, :, None] * eig_left, axis=0)
        return ((key_grad, value_grad, eig_right, weight_grad), (out_block, query_grad, left_term))

    initial = (
        jnp.zeros((node_count, heads_dev, head_size), jnp.float32),
        jnp.zeros((node_count, heads_dev, head_size), jnp.float32),
        jnp.zeros((heads_dev, eig_all.shape[0], node_count), jnp.float32),
        jnp.zeros(eig_weight.shape, jnp.float32),
    )
    totals, blocks = lax.scan(one_block, initial, jnp.arange(block_count))
    output_heads = blocks[0].reshape(node_count, head_width)
    query_grad_heads = blocks[1].reshape(node_count, head_width)
    key_grad_heads = (totals[0] * score_scale).astype(jnp.bfloat16).reshape(node_count, head_width)
    value_grad_heads = totals[1].astype(jnp.bfloat16).reshape(node_count, head_width)
    left_all = blocks[2].transpose(1, 0, 2).reshape(eig_all.shape[0], node_count)
    eig_term = left_all + jnp.sum(eig_weight[:, :, None] * totals[2], axis=0)
    returned = lax.all_to_all(
        jnp.stack([output_heads, query_grad_heads, key_grad_heads, value_grad_heads]),
        "node",
        split_axis=1,
        concat_axis=2,
        tiled=True,
    )
    output_nodes = returned[0]
    query_grad_nodes = returned[1]
    key_grad_nodes = returned[2]
    value_grad_nodes = returned[3]
    grad_rows = (
        jnp.einsum("re,de->rd", query_grad_nodes, w_query, preferred_element_type=jnp.float32)
        + jnp.einsum("re,de->rd", key_grad_nodes, w_key, preferred_element_type=jnp.float32)
        + jnp.einsum("re,de->rd", value_grad_nodes, w_value, preferred_element_type=jnp.float32)
    ).astype(jnp.bfloat16)
    grad_eigvec = lax.psum_scatter(eig_term, "node", scatter_dimension=1, tiled=True)
    grad_weight = lax.psum(totals[3], "clus")
    grad_terms = jnp.stack(
        [
            jnp.einsum(
                "rd,re->de", node_rows, query_grad_nodes, preferred_element_type=jnp.float32
            ),
            jnp.einsum("rd,re->de", node_rows, key_grad_nodes, preferred_element_type=jnp.float32),
            jnp.einsum(
                "rd,re->de", node_rows, value_grad_nodes, preferred_element_type=jnp.float32
            ),
            jnp.einsum("rd,re->de", grads_in, output_nodes, preferred_element_type=jnp.float32),
        ]
    )
    col_sums = lax.psum_scatter(grad_terms, "node", scatter_dimension=2, tiled=True)
    grad_proj = lax.psum_scatter(col_sums, "clus", scatter_dimension=1, tiled=True)
    return (grad_rows[None], grad_eigvec[None], grad_weight, grad_proj)


def solution(mesh):
    placed = (
        P("clus", "node", None),
        P("clus", "node", None),
        P(),
        P(),
        P(),
        P(),
        P("clus", None, None),
        P("node", None),
        P("clus", "node", None, None),
    )
    return jax.shard_map(
        body,
        mesh=mesh,
        in_specs=placed,
        out_specs=(
            P("clus", "node", None),
            P("clus", None, "node"),
            P("node", None),
            P(None, "clus", "node"),
        ),
        check_vma=False,
    )
```

profile of v0, /device:TPU:2, one launch (start us, length us, event | category | flops | bytes accessed | tf_op | source)
XLA Modules:
  0.0 431.4 jit_solution(2810686122069880913)
XLA Ops:
  7.2 1.5 copy-done
  8.8 1.8 fusion.53
  10.6 2.1 fusion.54
  13.8 1.4 copy.40
  15.3 7.5 %all-to-all-start = ((bf16[4,128,1024]{1,0,2:T(4,128)(2,1)}), bf16[4,128,1024]{1,0,2:T(4,128)(2,1)S(1)}, u32[]{:S(2)}, u32[]{:S(2)}) async-start(bf16[4,128,1024]{1,0,2:T(4,128)(2,1)} %copy.40), calls=%async_computation | async-start | bytes 2097152 | tf_op jit(solution)/shard_map/all_to_all | solution.py:16
  23.7 14.1 %all-to-all-done = bf16[4,128,1024]{1,0,2:T(4,128)(2,1)S(1)} async-done(((bf16[4,128,1024]{1,0,2:T(4,128)(2,1)}), bf16[4,128,1024]{1,0,2:T(4,128)(2,1)S(1)}, u32[]{:S(2)}, u32[]{:S(2)}) %all-to-all-start) | async-done | bytes 1048608 | tf_op jit(solution)/shard_map/all_to_all | solution.py:16
  41.4 74.0 %while.25 = (s32[]{:T(128)}, f32[2048,1,64]{0,2,1:T(8,128)}, f32[2048,1,64]{0,2,1:T(8,128)}, f32[1,64,2048]{2,1,0:T(8,128)}, f32[1,64]{1,0:T(1,128)S(1)}, /*inde...) while((s32[]{:T(128)}, f32[2048,1,64]{0,2,1:T(8,128)}, ...), condition=%wide.region_5.6_spmd.clone, body=%wide.region_0.5_spmd.clone.sunk | while | flops 1224702592 | bytes 83313016 | solution.py:101
  43.7 2.3 broadcast_in_dim.70
  46.0 1.7 fusion.131
  47.7 1.3 fusion.132
  50.0 1.3 fusion.134
  51.7 0.9 multiply_reduce_fusion.2
  52.6 1.4 fusion.141
  54.0 1.4 fusion.140
  57.3 2.3 fusion.136
  61.9 2.3 broadcast_in_dim.70
  64.2 1.7 fusion.131
  65.9 1.3 fusion.132
  68.2 1.3 fusion.134
  69.9 0.9 multiply_reduce_fusion.2
  70.8 1.4 fusion.141
  72.2 1.4 fusion.140
  74.2 0.9 bitcast_dynamic-update-slice_fusion.2
  75.6 2.6 fusion.136
  80.5 2.3 broadcast_in_dim.70
  82.8 1.7 fusion.131
  84.5 1.3 fusion.132
  86.8 1.3 fusion.134
  88.5 0.9 multiply_reduce_fusion.2
  89.4 1.4 fusion.141
  90.8 1.4 fusion.140
  92.8 0.9 bitcast_dynamic-update-slice_fusion.2
  94.2 2.6 fusion.136
  99.1 2.3 broadcast_in_dim.70
  101.4 1.7 fusion.131
  103.1 1.3 fusion.132
  105.4 1.3 fusion.134
  107.1 0.9 multiply_reduce_fusion.2
  108.0 1.4 fusion.141
  109.4 1.4 fusion.140
  111.4 0.8 bitcast_dynamic-update-slice_fusion.2
  112.8 2.6 fusion.136
  115.4 1.2 copy.46
  116.7 1.2 copy.47
  117.9 0.9 stack_reshape.13
  118.8 1.3 fusion.57
  120.0 1.1 pad_maximum_fusion.2
  121.1 2.5 copy.48
  123.6 4.4 %reshape.203 = bf16[16,2,16384]{2,1,0:T(2,128)(2,1)S(1)} reshape(bf16[2048,4,64]{2,1,0:T(4,128)(2,1)} %bitcast.283) | data formatting | bytes 2097152
  128.0 19.3 %all_to_all.30 = bf16[16,2,16384]{2,1,0:T(2,128)(2,1)} all-to-all(bf16[16,2,16384]{2,1,0:T(2,128)(2,1)S(1)} %reshape.203), channel_id=1, replica_groups=mesh['clus'=16,'node'=16] {'node'}, dimensions={0} | all-to-all | bytes 2097152 | tf_op jit(solution)/shard_map/all_to_all | solution.py:108
  147.3 5.2 %reshape.204 = bf16[2048,4,64]{2,1,0:T(4,128)(2,1)} reshape(bf16[16,2,16384]{2,1,0:T(2,128)(2,1)} %all_to_all.30) | data formatting | bytes 2097152
  152.6 2.8 copy.56
  158.7 6.0 %pad_maximum_fusion = f32[4,1024,1024]{1,2,0:T(8,128)} fusion(f32[1,1024,1024]{1,2,0:T(8,128)S(1)} %convolution_bitcast_fusion.4, f32[1,1024,1024]{1,2,0:T(8,128)S(1)} %convolution_bitcast_fusion.5, f32[1,1024,1024]{1,2,0:T(8,128)S(1)} %convolution_bitcast_fusion.6, f32[1,1024,1024]{1,2,0:T(8,128)S(1)} %convolution_bitcast_fusion.7), kind=kLoop, calls=%fused_computation.58 | loop fusion | flops 12582912 | bytes 33554432 | tf_op jit(solution)/shard_map/stack | solution.py:126
  164.8 116.6 %reduce-scatter.8.cloned.1.call-done = f32[4,1024,64]{1,2,0:T(8,128)} async-done(((f32[4,1024,1024]{1,2,0:T(8,128)}), f32[4,1024,64]{1,2,0:T(8,128)}) %reduce-scatter.8.cloned.1.call-update) | async-done | bytes 1048592 | tf_op jit(solution)/shard_map/reduce_scatter | solution.py:138
  281.4 2.7 copy.57
  284.1 3.2 reshape.201
  287.4 1.1 copy.60
  288.5 0.9 bitcast_add_fusion.1
  289.4 26.9 %psum.7 = f32[1,64]{1,0:T(1,128)} all-reduce(f32[1,64]{1,0:T(1,128)S(1)} %get-tuple-element.549), channel_id=1, replica_groups=mesh['clus'=16,'node'=16] {'clus'}, use_global_device_ids=true, to_apply=%region_7.8 | all-reduce | flops 64 | bytes 512 | tf_op jit(solution)/shard_map/psum | solution.py:125
  317.2 2.4 convolution_add_fusion.1
  319.6 1.6 fusion.52
  321.2 23.6 %reduce-scatter.10.cloned.1.call-done = f32[64,256]{1,0:T(8,128)} async-done(((f32[1024,256]{1,0:T(8,128)}), f32[64,256]{1,0:T(8,128)}) %reduce-scatter.10.cloned.1.call-update) | async-done | bytes 65552
  344.8 0.9 reshape.202
  346.4 78.4 %reduce-scatter.6.cloned.1.call-done = f32[64,128]{1,0:T(8,128)} async-done(((f32[64,2048]{1,0:T(8,128)}), f32[64,128]{1,0:T(8,128)}) %reduce-scatter.6.cloned.1.call-update) | async-done | bytes 32784 | tf_op jit(solution)/shard_map/reduce_scatter | solution.py:124
  (166 shorter events, 28.2 us)
Async XLA Ops:
  7.2 1.6 copy-start
  7.2 5.6 %copy-start.9 = (bf16[1,128,1024]{2,1,0:T(8,128)(2,1)S(1)}, bf16[1,128,1024]{2,1,0:T(8,128)(2,1)}, u32[]{:S(2)}) copy-start(bf16[1,128,1024]{2,1,0:T(8,128)(2,1)} %param.11) | copy-start | bytes 786436
  7.2 5.6 %copy-start.13 = (bf16[1024,1024]{1,0:T(8,128)(2,1)S(1)}, bf16[1024,1024]{1,0:T(8,128)(2,1)}, u32[]{:S(2)}) copy-start(bf16[1024,1024]{1,0:T(8,128)(2,1)} %param.15) | copy-start | bytes 6291460
  7.2 6.0 %copy-start.17 = (bf16[1,128,1024]{2,1,0:T(8,128)(2,1)S(1)}, bf16[1,128,1024]{2,1,0:T(8,128)(2,1)}, u32[]{:S(2)}) copy-start(bf16[1,128,1024]{2,1,0:T(8,128)(2,1)} %param.12) | copy-start | bytes 786436
  7.2 6.0 %copy-start.15 = (bf16[1024,1024]{1,0:T(8,128)(2,1)S(1)}, bf16[1024,1024]{1,0:T(8,128)(2,1)}, u32[]{:S(2)}) copy-start(bf16[1024,1024]{1,0:T(8,128)(2,1)} %param.16) | copy-start | bytes 6291460
  13.2 9.7 %copy-start.2 = (bf16[1,64,2048]{2,1,0:T(8,128)(2,1)S(1)}, bf16[1,64,2048]{2,1,0:T(8,128)(2,1)}, u32[]{:S(2)}) copy-start(bf16[1,64,2048]{2,1,0:T(8,128)(2,1)} %param.17) | copy-start | bytes 786436
  13.2 9.7 %copy-start.19 = (f32[1,64]{1,0:T(1,128)S(1)}, f32[1,64]{1,0:T(1,128)}, u32[]{:S(2)}) copy-start(f32[1,64]{1,0:T(1,128)} %param.18) | copy-start | bytes 772
  15.3 22.5 %all-to-all-start = ((bf16[4,128,1024]{1,0,2:T(4,128)(2,1)}), bf16[4,128,1024]{1,0,2:T(4,128)(2,1)S(1)}, u32[]{:S(2)}, u32[]{:S(2)}) async-start(bf16[4,128,1024]{1,0,2:T(4,128)(2,1)} %copy.40), calls=%async_computation | async-start | bytes 2097152 | tf_op jit(solution)/shard_map/all_to_all | solution.py:16
  22.8 258.6 %reduce-scatter.8.cloned.1.call-start = ((), (), s32[]{:S(2)}) async-start(), calls=%async_computation.6 | async-start | bytes 17825792 | tf_op jit(solution)/shard_map/reduce_scatter | solution.py:138
  46.0 1.7 copy-start.1
  46.0 1.7 copy-start.3
  46.0 1.7 copy-start.11
  49.0 1.0 copy-start.12
  49.0 1.0 copy-start.16
  51.7 3.7 copy-start.4
  54.0 2.8 copy-start.6
  55.9 3.7 copy-start.5
  57.3 2.3 copy-start.7
  64.2 1.7 copy-start.1
  64.2 1.7 copy-start.3
  64.2 1.7 copy-start.11
  67.2 1.0 copy-start.12
  67.2 1.0 copy-start.16
  69.9 3.7 copy-start.4
  72.2 2.8 copy-start.6
  74.2 4.1 copy-start.5
  75.6 2.6 copy-start.7
  82.8 1.7 copy-start.1
  82.8 1.7 copy-start.3
  82.8 1.7 copy-start.11
  85.8 1.0 copy-start.12
  85.8 1.0 copy-start.16
  88.5 3.7 copy-start.4
  90.8 2.8 copy-start.6
  92.8 4.0 copy-start.5
  94.2 2.6 copy-start.7
  101.4 1.7 copy-start.1
  101.4 1.7 copy-start.3
  101.4 1.7 copy-start.11
  104.4 1.0 copy-start.12
  104.4 1.0 copy-start.16
  107.1 3.7 copy-start.4
  109.4 2.8 copy-start.6
  111.4 4.0 copy-start.5
  112.8 2.6 copy-start.7
  152.6 3.3 copy-start.10
  156.6 1.4 copy-start.18
  164.7 123.8 %copy-start.8 = (f32[1,64,2048]{2,1,0:T(8,128)S(1)}, f32[1,64,2048]{2,1,0:T(8,128)}, u32[]{:S(2)}) copy-start(f32[1,64,2048]{2,1,0:T(8,128)} %get-tuple-element.548) | copy-start | bytes 1572868
  164.7 180.1 %reduce-scatter.10.cloned.1.call-start = ((), (), s32[]{:S(2)}) async-start(), calls=%async_computation.7 | async-start | bytes 1114112
  287.4 137.5 %reduce-scatter.6.cloned.1.call-start = ((), (), s32[]{:S(2)}) async-start(), calls=%async_computation.5 | async-start | bytes 557056 | tf_op jit(solution)/shard_map/reduce_scatter | solution.py:124
  316.4 3.3 copy-start.14
Sparse Core Ops, SparseCore 0:
  164.8 116.5 reduce-scatter.7
  287.5 57.2 reduce-scatter.9
  349.3 75.5 reduce-scatter.5
where the time goes:
time: 433 us; the launch traced here: 431 us
  waiting for transfers between devices  233 us (54%)
  matrix products  58.3 us (13%)
  local copies, waits for them, and re-layouts  48.1 us (11%)
  blocking collectives  46.2 us (11%)
  other arithmetic  21.1 us (5%)
  between operations  14.2 us (3%)
  starting transfers between devices  7.6 us (2%)
    reduce_scatter x1, waiting for transfers between devices, body(): lax.psum_scatter(grad_terms, 'node', scatter_dimension=2, tiled=True)  117 us
    reduce_scatter x1, waiting for transfers between devices, body(): lax.psum_scatter(eig_term, 'node', scatter_dimension=1, tiled=True)  78.4 us
    psum x1, blocking collectives, body(): grad_weight = lax.psum(totals[3], 'clus')  26.9 us
    unnamed x4, waiting for transfers between devices  23.7 us
    all_to_all x1, blocking collectives, body(): lax.all_to_all(jnp.stack([output_heads, query_grad_heads, key_grad_heads,...  19.3 us
    unnamed x28, local copies, waits for them, and re-layouts  18.8 us
    all_to_all x1, waiting for transfers between devices, body(): lax.all_to_all(jnp.stack([query, keys_local, values_local, d_att]), 'node...  14.1 us
    broadcast_in_dim x8, local copies, waits for them, and re-layouts, one_block(): jnp.broadcast_to(tile_rows[:, :, None, :, None] > 0, (heads_dev, block_ro...  10.5 us
  transfers between devices with their start and end apart: 4, of which 4 were waited for; matrix products, arithmetic and copies ran while one was open for 2% of the time, Pallas kernels for 0%

commit v1 on v0

--- a/solution.py
+++ b/solution.py
@@ -105,12 +105,14 @@
     value_grad_heads = totals[1].astype(jnp.bfloat16).reshape(node_count, head_width)
     left_all = blocks[2].transpose(1, 0, 2).reshape(eig_all.shape[0], node_count)
     eig_term = left_all + jnp.sum(eig_weight[:, :, None] * totals[2], axis=0)
-    returned = lax.all_to_all(
-        jnp.stack([output_heads, query_grad_heads, key_grad_heads, value_grad_heads]),
-        "node",
-        split_axis=1,
-        concat_axis=2,
-        tiled=True,
+    place_the_seats_all = lambda local_x, out_dim, axis_k: jnp.concatenate(
+        lax.all_to_all(
+            jnp.stack(jnp.split(local_x, lax.axis_size("node"), out_dim), 0), "node", 0, 0
+        ),
+        axis_k,
+    )
+    returned = place_the_seats_all(
+        jnp.stack([output_heads, query_grad_heads, key_grad_heads, value_grad_heads]), 1, axis_k=2
     )
     output_nodes = returned[0]
     query_grad_nodes = returned[1]

time: 433 us -> 416 us (0.961)
  local copies, waits for them, and re-layouts: 48.1 us -> 32.6 us
    unnamed x28 -> x41, local copies, waits for them, and re-layouts: 18.8 us -> 9.58 us
where the time goes in v1:
time: 416 us; the launch traced here: 415 us
  waiting for transfers between devices  233 us (56%)
  matrix products  58.3 us (14%)
  blocking collectives  46.1 us (11%)
  local copies, waits for them, and re-layouts  32.6 us (8%)
  other arithmetic  20.1 us (5%)
  between operations  14.2 us (3%)
  starting transfers between devices  7.6 us (2%)
    reduce_scatter x1, waiting for transfers between devices, body(): lax.psum_scatter(grad_terms, 'node', scatter_dimension=2, tiled=True)  117 us
    reduce_scatter x1, waiting for transfers between devices, body(): lax.psum_scatter(eig_term, 'node', scatter_dimension=1, tiled=True)  78.6 us
    psum x1, blocking collectives, body(): grad_weight = lax.psum(totals[3], 'clus')  26.9 us
    unnamed x4, waiting for transfers between devices  23.6 us
    all_to_all x1, blocking collectives, body(): lax.all_to_all(jnp.stack(jnp.split(local_x, lax.axis_size('node'), out_di...  19.2 us
    all_to_all x1, waiting for transfers between devices, body(): lax.all_to_all(jnp.stack([query, keys_local, values_local, d_att]), 'node...  14.1 us
    broadcast_in_dim x8, local copies, waits for them, and re-layouts, one_block(): jnp.broadcast_to(tile_rows[:, :, None, :, None] > 0, (heads_dev, block_ro...  10.5 us
    dot_general x4, matrix products, one_block(): jnp.einsum('hij,ihd->jhd', dscore, query_block, preferred_element_type=jn...  10.1 us
  transfers between devices with their start and end apart: 4, of which 4 were waited for; matrix products, arithmetic and copies ran while one was open for 2% of the time, Pallas kernels for 0%

profile of v1, /device:TPU:2, one launch (start us, length us, event | category | flops | bytes accessed | tf_op | source)
XLA Modules:
  0.0 414.9 jit_solution(9513065504960201619)
XLA Ops:
  7.2 1.5 copy-done
  8.8 1.8 fusion.53
  10.6 2.1 fusion.54
  13.8 1.4 copy.28
  15.3 7.5 %all-to-all-start = ((bf16[4,128,1024]{1,0,2:T(4,128)(2,1)}), bf16[4,128,1024]{1,0,2:T(4,128)(2,1)S(1)}, u32[]{:S(2)}, u32[]{:S(2)}) async-start(bf16[4,128,1024]{1,0,2:T(4,128)(2,1)} %copy.28), calls=%async_computation | async-start | bytes 2097152 | tf_op jit(solution)/shard_map/all_to_all | solution.py:16
  22.9 0.8 multiply_convert_fusion.1
  23.7 14.1 %all-to-all-done = bf16[4,128,1024]{1,0,2:T(4,128)(2,1)S(1)} async-done(((bf16[4,128,1024]{1,0,2:T(4,128)(2,1)}), bf16[4,128,1024]{1,0,2:T(4,128)(2,1)S(1)}, u32[]{:S(2)}, u32[]{:S(2)}) %all-to-all-start) | async-done | bytes 1048608 | tf_op jit(solution)/shard_map/all_to_all | solution.py:16
  38.2 0.8 squeeze.48
  39.2 0.8 squeeze.47
  40.5 0.8 squeeze.43
  41.4 74.0 %while.25 = (s32[]{:T(128)}, f32[2048,1,64]{0,2,1:T(8,128)}, f32[2048,1,64]{0,2,1:T(8,128)}, f32[1,64,2048]{2,1,0:T(8,128)}, f32[1,64]{1,0:T(1,128)S(1)}, /*inde...) while((s32[]{:T(128)}, f32[2048,1,64]{0,2,1:T(8,128)}, ...), condition=%wide.region_5.6_spmd.clone, body=%wide.region_0.5_spmd.clone.sunk | while | flops 1224702592 | bytes 83313016 | solution.py:101
  43.7 2.3 broadcast_in_dim.70
  46.0 1.7 fusion.147
  47.7 1.3 fusion.148
  50.0 1.3 fusion.150
  51.7 0.9 multiply_reduce_fusion.2
  52.6 1.4 fusion.157
  54.0 1.4 fusion.156
  55.9 0.8 bitcast_dynamic-update-slice_fusion.2
  57.3 2.3 fusion.152
  61.9 2.3 broadcast_in_dim.70
  64.2 1.7 fusion.147
  65.9 1.3 fusion.148
  68.2 1.3 fusion.150
  69.9 0.9 multiply_reduce_fusion.2
  70.8 1.4 fusion.157
  72.2 1.4 fusion.156
  74.2 0.9 bitcast_dynamic-update-slice_fusion.2
  75.6 2.6 fusion.152
  80.5 2.3 broadcast_in_dim.70
  82.8 1.7 fusion.147
  84.5 1.3 fusion.148
  86.8 1.3 fusion.150
  88.5 0.9 multiply_reduce_fusion.2
  89.4 1.4 fusion.157
  90.8 1.4 fusion.156
  92.8 0.9 bitcast_dynamic-update-slice_fusion.2
  94.2 2.6 fusion.152
  99.1 2.3 broadcast_in_dim.70
  101.4 1.7 fusion.147
  103.1 1.3 fusion.148
  105.4 1.3 fusion.150
  107.1 0.9 multiply_reduce_fusion.2
  108.0 1.4 fusion.157
  109.4 1.4 fusion.156
  111.4 0.8 bitcast_dynamic-update-slice_fusion.2
  112.8 2.6 fusion.152
  115.4 1.2 copy.34
  116.7 1.2 copy.35
  118.1 1.3 fusion.57
  120.0 19.2 %all_to_all.20 = bf16[16,4,128,64]{2,3,1,0:T(8,128)(2,1)S(1)} all-to-all(bf16[16,4,128,64]{2,3,1,0:T(8,128)(2,1)S(1)} %fusion.66), channel_id=1, replica_groups=mesh['clus'=16,'node'=16] {'node'}, dimensions={0} | all-to-all | bytes 2097152 | tf_op jit(solution)/shard_map/all_to_all | solution.py:109
  142.1 6.0 %pad_maximum_fusion = f32[4,1024,1024]{1,2,0:T(8,128)} fusion(f32[1,1024,1024]{1,2,0:T(8,128)S(1)} %convolution_bitcast_fusion.4, f32[1,1024,1024]{1,2,0:T(8,128)S(1)} %convolution_bitcast_fusion.5, f32[1,1024,1024]{1,2,0:T(8,128)S(1)} %convolution_bitcast_fusion.6, f32[1,1024,1024]{1,2,0:T(8,128)S(1)} %convolution_bitcast_fusion.7), kind=kLoop, calls=%fused_computation.58 | loop fusion | flops 12582912 | bytes 33554432 | tf_op jit(solution)/shard_map/stack | solution.py:128
  148.2 116.6 %reduce-scatter.8.cloned.1.call-done = f32[4,1024,64]{1,2,0:T(8,128)} async-done(((f32[4,1024,1024]{1,2,0:T(8,128)}), f32[4,1024,64]{1,2,0:T(8,128)}) %reduce-scatter.8.cloned.1.call-update) | async-done | bytes 1048592 | tf_op jit(solution)/shard_map/reduce_scatter | solution.py:140
  264.9 2.7 copy.38
  267.6 3.2 reshape.206
  270.9 1.1 copy.41
  272.0 0.9 bitcast_add_fusion.1
  272.9 26.9 %psum.7 = f32[1,64]{1,0:T(1,128)} all-reduce(f32[1,64]{1,0:T(1,128)S(1)} %get-tuple-element.545), channel_id=1, replica_groups=mesh['clus'=16,'node'=16] {'clus'}, use_global_device_ids=true, to_apply=%region_7.8 | all-reduce | flops 64 | bytes 512 | tf_op jit(solution)/shard_map/psum | solution.py:127
  299.8 0.8 fusion.86
  300.6 2.4 convolution_add_fusion.1
  303.1 1.6 fusion.52
  304.6 23.5 %reduce-scatter.10.cloned.1.call-done = f32[64,256]{1,0:T(8,128)} async-done(((f32[1024,256]{1,0:T(8,128)}), f32[64,256]{1,0:T(8,128)}) %reduce-scatter.10.cloned.1.call-update) | async-done | bytes 65552
  328.2 0.9 reshape.207
  329.8 78.6 %reduce-scatter.6.cloned.1.call-done = f32[64,128]{1,0:T(8,128)} async-done(((f32[64,2048]{1,0:T(8,128)}), f32[64,128]{1,0:T(8,128)}) %reduce-scatter.6.cloned.1.call-update) | async-done | bytes 32784 | tf_op jit(solution)/shard_map/reduce_scatter | solution.py:126
  (174 shorter events, 23.6 us)
Async XLA Ops:
  7.2 1.6 copy-start
  7.2 5.6 %copy-start.9 = (bf16[1,128,1024]{2,1,0:T(8,128)(2,1)S(1)}, bf16[1,128,1024]{2,1,0:T(8,128)(2,1)}, u32[]{:S(2)}) copy-start(bf16[1,128,1024]{2,1,0:T(8,128)(2,1)} %param.11) | copy-start | bytes 786436
  7.2 5.6 %copy-start.13 = (bf16[1024,1024]{1,0:T(8,128)(2,1)S(1)}, bf16[1024,1024]{1,0:T(8,128)(2,1)}, u32[]{:S(2)}) copy-start(bf16[1024,1024]{1,0:T(8,128)(2,1)} %param.15) | copy-start | bytes 6291460
  7.2 6.0 %copy-start.17 = (bf16[1,128,1024]{2,1,0:T(8,128)(2,1)S(1)}, bf16[1,128,1024]{2,1,0:T(8,128)(2,1)}, u32[]{:S(2)}) copy-start(bf16[1,128,1024]{2,1,0:T(8,128)(2,1)} %param.12) | copy-start | bytes 786436
  7.2 6.0 %copy-start.15 = (bf16[1024,1024]{1,0:T(8,128)(2,1)S(1)}, bf16[1024,1024]{1,0:T(8,128)(2,1)}, u32[]{:S(2)}) copy-start(bf16[1024,1024]{1,0:T(8,128)(2,1)} %param.16) | copy-start | bytes 6291460
  13.2 9.7 %copy-start.2 = (bf16[1,64,2048]{2,1,0:T(8,128)(2,1)S(1)}, bf16[1,64,2048]{2,1,0:T(8,128)(2,1)}, u32[]{:S(2)}) copy-start(bf16[1,64,2048]{2,1,0:T(8,128)(2,1)} %param.17) | copy-start | bytes 786436
  13.2 9.7 %copy-start.19 = (f32[1,64]{1,0:T(1,128)S(1)}, f32[1,64]{1,0:T(1,128)}, u32[]{:S(2)}) copy-start(f32[1,64]{1,0:T(1,128)} %param.18) | copy-start | bytes 772
  15.3 22.5 %all-to-all-start = ((bf16[4,128,1024]{1,0,2:T(4,128)(2,1)}), bf16[4,128,1024]{1,0,2:T(4,128)(2,1)S(1)}, u32[]{:S(2)}, u32[]{:S(2)}) async-start(bf16[4,128,1024]{1,0,2:T(4,128)(2,1)} %copy.28), calls=%async_computation | async-start | bytes 2097152 | tf_op jit(solution)/shard_map/all_to_all | solution.py:16
  22.8 242.1 %reduce-scatter.8.cloned.1.call-start = ((), (), s32[]{:S(2)}) async-start(), calls=%async_computation.6 | async-start | bytes 17825792 | tf_op jit(solution)/shard_map/reduce_scatter | solution.py:140
  46.0 1.7 copy-start.1
  46.0 1.7 copy-start.3
  46.0 1.7 copy-start.11
  49.0 1.0 copy-start.12
  49.0 1.0 copy-start.16
  51.7 3.7 copy-start.4
  54.0 2.8 copy-start.6
  55.9 3.7 copy-start.5
  57.3 2.3 copy-start.7
  64.2 1.7 copy-start.1
  64.2 1.7 copy-start.3
  64.2 1.7 copy-start.11
  67.2 1.0 copy-start.12
  67.2 1.0 copy-start.16
  69.9 3.7 copy-start.4
  72.2 2.8 copy-start.6
  74.2 4.1 copy-start.5
  75.6 2.6 copy-start.7
  82.8 1.7 copy-start.1
  82.8 1.7 copy-start.3
  82.8 1.7 copy-start.11
  85.8 1.0 copy-start.12
  85.8 1.0 copy-start.16
  88.5 3.7 copy-start.4
  90.8 2.8 copy-start.6
  92.8 4.0 copy-start.5
  94.2 2.6 copy-start.7
  101.4 1.7 copy-start.1
  101.4 1.7 copy-start.3
  101.4 1.7 copy-start.11
  104.4 1.0 copy-start.12
  104.4 1.0 copy-start.16
  107.1 3.7 copy-start.4
  109.4 2.8 copy-start.6
  111.4 4.0 copy-start.5
  112.8 2.6 copy-start.7
  119.3 20.0 %copy-start.10 = (bf16[1,128,1024]{2,1,0:T(8,128)(2,1)S(1)}, bf16[1,128,1024]{2,1,0:T(8,128)(2,1)}, u32[]{:S(2)}) copy-start(bf16[1,128,1024]{2,1,0:T(8,128)(2,1)} %param.11) | copy-start | bytes 786436
  140.0 1.4 copy-start.18
  148.2 123.8 %copy-start.8 = (f32[1,64,2048]{2,1,0:T(8,128)S(1)}, f32[1,64,2048]{2,1,0:T(8,128)}, u32[]{:S(2)}) copy-start(f32[1,64,2048]{2,1,0:T(8,128)} %get-tuple-element.544) | copy-start | bytes 1572868
  148.2 180.0 %reduce-scatter.10.cloned.1.call-start = ((), (), s32[]{:S(2)}) async-start(), calls=%async_computation.7 | async-start | bytes 1114112
  270.9 137.5 %reduce-scatter.6.cloned.1.call-start = ((), (), s32[]{:S(2)}) async-start(), calls=%async_computation.5 | async-start | bytes 557056 | tf_op jit(solution)/shard_map/reduce_scatter | solution.py:126
  299.8 3.3 copy-start.14
Sparse Core Ops, SparseCore 0:
  148.3 116.5 reduce-scatter.7
  271.0 57.1 reduce-scatter.9
  332.6 75.7 reduce-scatter.5
